TPU v7x, 32 devices: a whole 2x2x4 slice. The times are simulated.
32 devices in a mesh: tm: 8 (over z, core), space: 4 (over y, x).
Axes of the slice: x: 2, y: 2, z: 4, core: 2. Of those that a mesh axis runs over, the one named last changes fastest.
Arguments:
- increment: float32 [8, 4, 137, 512], P('tm', None, None, 'space'), may hold values from -26 to 26
- courant: float32 [8, 4, 137, 512], P('tm', None, None, 'space'), may hold values from -0.9 to 0.9
- error_weight: float32 [4, 137], replicated, may hold values from 0.5 to 2
- obs_code: int32 [8, 4, 4, 128], P('tm', 'space'), may hold values from 0 to 280574, as said below
- obs_values: float32 [8, 4, 4, 3, 128], P('tm', 'space'), as said below
- obs_count: int32 [8, 4, 4], P('tm', 'space'), may hold values from 25 to 128, as said below
Outputs:
- new_increment: float32 [8, 4, 137, 512], P('tm', None, None, 'space')
- departures: float32 [8, 4, 4, 128], P('tm', 'space')
Inputs may be any that keep to these rules, and one draw needn't show every extreme that they name: `obs_code`: code = ((t * 4 + f) * 137 + l) * 128 + c for an observation of the state after step t + 1 of its sub-window, field f, level l, between columns c and c + 1 of the destination tile, c < 127; slots at or beyond the count carry no observation. `obs_values`: row 1 lies in [0, 1], row 2 in [0.5, 4]. `obs_count`: in every sub-window some destination tile receives 128 observations from every source tile.
All inputs are finite; a program needn't handle non-finite values.
Results may differ from a plain program's by a relative error of at most 0.0003.
Values sent between devices are 32-bit elements; how exact they have to be, the bound alone decides.
A program may use at most 64 MiB of HBM per device.

v0:
```python
import jax
import jax.numpy as jnp
from jax import lax
from jax.sharding import PartitionSpec as P


def padded_2(array, sides, width):
    for axis, dim in sides:
        size, length = (lax.axis_size(axis), array.shape[dim])
        up = [(i, (i + 1) % size) for i in range(size)]
        down = [(j, i) for i, j in up]
        last = lax.slice_in_dim(array, length - width, length, axis=dim)
        initial = lax.slice_in_dim(array, 0, width, axis=dim)
        before = lax.ppermute(last, axis, up)
        after = lax.ppermute(initial, axis, down)
        array = jnp.concatenate([before, array, after], axis=dim)
    return array


def passed_along(array, axis, by):
    size = lax.axis_size(axis)
    pairs = [(i, i + by) for i in range(size) if 0 <= i + by < size]
    return lax.ppermute(array, axis, pairs)


def on_device(increment, courant, error_weight, obs_code, obs_values, obs_count):
    start = increment[0]
    cour = courant[0]
    steps = cour.shape[0]
    per_state = start.size
    slots = obs_code.shape[-1]
    qinv = error_weight[:, :, None]
    code_in, values_in, count_in = (
        lax.all_to_all(obs_code, "space", split_axis=2, concat_axis=2, tiled=True),
        lax.all_to_all(obs_values, "space", split_axis=2, concat_axis=2, tiled=True),
        lax.all_to_all(obs_count, "space", split_axis=2, concat_axis=2, tiled=True),
    )
    code_in = code_in[0, 0]
    values_in = values_in[0, 0]
    flat = code_in % per_state
    when = code_in // per_state
    valid = jnp.arange(slots, dtype=jnp.int32)[None, :] < count_in[0, 0][:, None]
    innovation = values_in[:, 0, :]
    weight = values_in[:, 1, :]
    rinv = values_in[:, 2, :]
    margin = 1
    cour_pad = padded_2(cour, (("space", 2),), margin)
    left_pad = 0.5 * cour_pad * (1.0 + cour_pad)
    right_pad = 0.5 * cour_pad * (cour_pad - 1.0)
    centre = 1.0 - cour * cour
    seen_all = jnp.zeros(flat.shape, jnp.float32)
    left = left_pad[:, :, 1:-1]
    right = right_pad[:, :, 1:-1]
    state = start
    for step in range(steps):
        padded = padded_2(state, (("space", 2),), 1)
        state = (
            centre[step] * state + left[step] * padded[:, :, :-2] + right[step] * padded[:, :, 2:]
        )
        line = state.reshape(-1)
        seen = weight * line[flat] + (1.0 - weight) * line[flat + 1]
        seen_all = jnp.where(when == step, seen, seen_all)
    departed = jnp.where(valid, seen_all - innovation, 0.0)
    pushed = rinv * departed
    previous = passed_along(state, "tm", 1)
    jump_own = start - previous
    weighted_own = qinv * jump_own
    weighted_next = passed_along(weighted_own, "tm", -1)
    jump_part = jnp.sum(weighted_own * jump_own)
    target = when * per_state + flat
    forcing = jnp.zeros((steps * per_state,), jnp.float32)
    forcing = forcing.at[target].add(weight * pushed).at[target + 1].add((1.0 - weight) * pushed)
    forcing = forcing.reshape((steps,) + start.shape)
    lam = -weighted_next + forcing[steps - 1]
    for step in reversed(range(steps)):
        retreat_padded = padded_2(lam, (("space", 2),), 1)
        lam = (
            centre[step] * lam
            + left_pad[step][:, 2:] * retreat_padded[:, :, 2:]
            + right_pad[step][:, :-2] * retreat_padded[:, :, :-2]
        )
        if step > 0:
            lam = lam + forcing[step - 1]
    gradient = weighted_own + lam
    cost_part = 0.5 * (jump_part + jnp.sum(pushed * departed))
    norm_part = jnp.sum(gradient * gradient)
    cost, norm = lax.psum((cost_part, norm_part), ("tm", "space"))
    renewed = increment - cost / norm * gradient[None]
    returned = lax.all_to_all(
        departed[None, None], "space", split_axis=2, concat_axis=2, tiled=True
    )
    return (renewed, returned)


def solution(mesh):
    in_specs = (
        P("tm", None, None, "space"),
        P("tm", None, None, "space"),
        P(),
        P("tm", "space", None, None),
        P("tm", "space", None, None, None),
        P("tm", "space", None),
    )
    out_specs = (P("tm", None, None, "space"), P("tm", "space", None, None))
    return jax.shard_map(
        on_device, mesh=mesh, in_specs=in_specs, out_specs=out_specs, check_vma=False
    )
```

profile of v0, /device:TPU:0, one launch (start us, length us, event | category | flops | bytes accessed | tf_op | source)
XLA Modules:
  0.0 220.6 jit_solution(10533462246855914328)
XLA Ops:
  1.9 5.2 %all-to-all-start.1 = ((s32[1,1,4]{1,0,2:T(1,128)}), s32[1,1,4]{1,0,2:T(1,128)S(1)}, u32[]{:S(2)}, u32[]{:S(2)}) async-start(s32[1,1,4]{1,0,2:T(1,128)} %copy.83), calls=%async_computation.1 | async-start | bytes 4096 | tf_op jit(solution)/shard_map/all_to_all | solution.py:36
  8.3 2.1 collective-permute-start
  14.3 1.9 collective-permute-start.3
  16.2 3.2 %all-to-all-start.2 = ((s32[1,1,4,128]{3,1,0,2:T(1,128)}), s32[1,1,4,128]{3,1,0,2:T(1,128)S(1)}, u32[]{:S(2)}, u32[]{:S(2)}) async-start(s32[1,1,4,128]{3,1,0,2:T(1,128)} %bitcast.16), calls=%async_computation.2 | async-start | bytes 4096 | tf_op jit(solution)/shard_map/all_to_all | solution.py:34
  20.7 8.2 %all-to-all-done.2 = s32[1,1,4,128]{3,1,0,2:T(1,128)S(1)} async-done(((s32[1,1,4,128]{3,1,0,2:T(1,128)}), s32[1,1,4,128]{3,1,0,2:T(1,128)S(1)}, u32[]{:S(2)}, u32[]{:S(2)}) %all-to-all-start.2) | async-done | bytes 2080 | tf_op jit(solution)/shard_map/all_to_all | solution.py:34
  28.9 3.2 %all-to-all-start = ((f32[1,1,4,3,128]{4,3,1,0,2:T(4,128)}), f32[1,1,4,3,128]{4,3,1,0,2:T(4,128)S(1)}, u32[]{:S(2)}, u32[]{:S(2)}) async-start(f32[1,1,4,3,128]{4,3,1,0,2:T(4,128)} %copy.81), calls=%async_computation | async-start | bytes 16384 | tf_op jit(solution)/shard_map/all_to_all | solution.py:35
  34.1 2.0 collective-permute-start.4
  37.3 7.6 %collective-permute-done.4 = f32[4,137,1]{2,1,0:T(8,128)S(1)} collective-permute-done((f32[4,137,1]{2,1,0:T(8,128)S(1)}, f32[4,137,1]{2,1,0:T(8,128)S(1)}, u32[]{:S(2)}, u32[]{:S(2)}) %collective-permute-start.4) | collective-permute-done | bytes 2224 | tf_op jit(solution)/shard_map/ppermute | solution.py:14
  44.9 3.5 %collective-permute-done.5 = f32[4,137,1]{2,1,0:T(8,128)} collective-permute-done((f32[4,137,1]{2,1,0:T(8,128)S(1)}, f32[4,137,1]{2,1,0:T(8,128)}, u32[]{:S(2)}, u32[]{:S(2)}) %collective-permute-start.5) | collective-permute-done | bytes 2224 | tf_op jit(solution)/shard_map/ppermute | solution.py:15
  54.0 3.1 %gather_fusion.7 = f32[512]{0:T(512)S(1)} fusion(f32[70144]{0:T(1024)S(1)} %reshape.355, s32[1024]{0:T(1024)S(1)} %get-tuple-element.72), kind=kCustom, calls=%fused_computation.7 | custom fusion | bytes 6144 | tf_op jit(solution)/shard_map/gather | solution.py:61
  57.1 3.1 %gather_fusion.6 = f32[512]{0:T(512)S(1)} fusion(f32[70144]{0:T(1024)S(1)} %reshape.355, s32[1024]{0:T(1024)S(1)} %get-tuple-element.73), kind=kCustom, calls=%fused_computation.6 | custom fusion | bytes 6144 | tf_op jit(solution)/shard_map/gather | solution.py:61
  60.3 3.1 %gather_fusion.5 = f32[512]{0:T(512)S(1)} fusion(f32[70144]{0:T(1024)S(1)} %reshape.354, s32[1024]{0:T(1024)S(1)} %get-tuple-element.72), kind=kCustom, calls=%fused_computation.5 | custom fusion | bytes 6144 | tf_op jit(solution)/shard_map/gather | solution.py:61
  63.5 3.1 %gather_fusion.4 = f32[512]{0:T(512)S(1)} fusion(f32[70144]{0:T(1024)S(1)} %reshape.354, s32[1024]{0:T(1024)S(1)} %get-tuple-element.73), kind=kCustom, calls=%fused_computation.4 | custom fusion | bytes 6144 | tf_op jit(solution)/shard_map/gather | solution.py:61
  68.7 2.4 %collective-permute-start.9 = (f32[4,137,1]{2,1,0:T(8,128)S(1)}, f32[4,137,1]{2,1,0:T(8,128)S(1)}, u32[]{:S(2)}, u32[]{:S(2)}) collective-permute-start(f32[4,137,1]{2,1,0:T(8,128)S(1)} %get-tuple-element.56), channel_id=1, source_target_pairs={{1,0},{2,1},{3,2},{0,3},{5,4},{6,5},{7,6},{4,7},{9,8},{10,9},{11,1... | collective-permute-start | bytes 6584 | tf_op jit(solution)/shard_map/ppermute | solution.py:15
  71.1 3.1 %gather_fusion.3 = f32[512]{0:T(512)S(1)} fusion(f32[70144]{0:T(1024)S(1)} %reshape.353, s32[1024]{0:T(1024)S(1)} %get-tuple-element.72), kind=kCustom, calls=%fused_computation.3 | custom fusion | bytes 6144 | tf_op jit(solution)/shard_map/gather | solution.py:61
  74.2 3.1 %gather_fusion.2 = f32[512]{0:T(512)S(1)} fusion(f32[70144]{0:T(1024)S(1)} %reshape.353, s32[1024]{0:T(1024)S(1)} %get-tuple-element.73), kind=kCustom, calls=%fused_computation.2 | custom fusion | bytes 6144 | tf_op jit(solution)/shard_map/gather | solution.py:61
  77.4 1.9 collective-permute-done.9
  79.7 3.1 %gather_fusion.1 = f32[512]{0:T(512)S(1)} fusion(f32[70144]{0:T(1024)S(1)} %reshape.352, s32[1024]{0:T(1024)S(1)} %get-tuple-element.72), kind=kCustom, calls=%fused_computation.1 | custom fusion | bytes 6144 | tf_op jit(solution)/shard_map/gather | solution.py:61
  82.8 3.1 %gather_fusion = f32[512]{0:T(512)S(1)} fusion(f32[70144]{0:T(1024)S(1)} %reshape.352, s32[1024]{0:T(1024)S(1)} %get-tuple-element.73), kind=kCustom, calls=%fused_computation | custom fusion | bytes 6144 | tf_op jit(solution)/shard_map/gather | solution.py:61
  88.7 3.5 %scatter_custom_fusion = f32[280576]{0:T(1024)S(1)} fusion(s32[512]{0:T(512)S(1)} %fusion.42, f32[512]{0:T(512)S(1)} %get-tuple-element.67, f32[]{:T(128)} %constant.16.clone.1), kind=kCustom, calls=%fused_computation.10 | custom fusion | flops 512 | bytes 1122308 | tf_op jit(solution)/shard_map/scatter-add | solution.py:72
  92.2 3.7 %scatter_fusion = f32[280576]{0:T(1024)S(1)} fusion(f32[280576]{0:T(1024)S(1)} %scatter_custom_fusion, s32[512]{0:T(512)S(1)} %get-tuple-element.70, f32[512]{0:T(512)S(1)} %get-tuple-element.66), kind=kCustom, calls=%fused_computation.9 | custom fusion | flops 512 | bytes 8192 | tf_op jit(solution)/shard_map/scatter-add | solution.py:72
  100.0 2.4 %collective-permute-done.11 = f32[4,137,128]{2,1,0:T(8,128)} collective-permute-done((f32[4,137,128]{2,1,0:T(8,128)}, f32[4,137,128]{2,1,0:T(8,128)}, u32[]{:S(2)}, u32[]{:S(2)}) %collective-permute-start.11) | collective-permute-done | bytes 280608 | tf_op jit(solution)/shard_map/ppermute | solution.py:23
  108.4 3.0 %collective-permute-done.12 = f32[4,137,1]{2,1,0:T(8,128)} collective-permute-done((f32[4,137,1]{2,1,0:T(8,128)}, f32[4,137,1]{2,1,0:T(8,128)}, u32[]{:S(2)}, u32[]{:S(2)}) %collective-permute-start.12) | collective-permute-done | bytes 2224 | tf_op jit(solution)/shard_map/ppermute | solution.py:15
  111.4 6.2 %collective-permute-done.13 = f32[4,137,1]{2,1,0:T(8,128)} collective-permute-done((f32[4,137,1]{2,1,0:T(8,128)}, f32[4,137,1]{2,1,0:T(8,128)}, u32[]{:S(2)}, u32[]{:S(2)}) %collective-permute-start.13) | collective-permute-done | bytes 2224 | tf_op jit(solution)/shard_map/ppermute | solution.py:14
  120.2 1.7 collective-permute-start.15
  122.2 4.7 %collective-permute-done.14 = f32[4,137,1]{2,1,0:T(8,128)S(1)} collective-permute-done((f32[4,137,1]{2,1,0:T(8,128)}, f32[4,137,1]{2,1,0:T(8,128)S(1)}, u32[]{:S(2)}, u32[]{:S(2)}) %collective-permute-start.14) | collective-permute-done | bytes 2224 | tf_op jit(solution)/shard_map/ppermute | solution.py:15
  126.9 6.5 %collective-permute-done.15 = f32[4,137,1]{2,1,0:T(8,128)} collective-permute-done((f32[4,137,1]{2,1,0:T(8,128)}, f32[4,137,1]{2,1,0:T(8,128)}, u32[]{:S(2)}, u32[]{:S(2)}) %collective-permute-start.15) | collective-permute-done | bytes 2224 | tf_op jit(solution)/shard_map/ppermute | solution.py:14
  137.9 5.8 %collective-permute-done.16 = f32[4,137,1]{2,1,0:T(8,128)S(1)} collective-permute-done((f32[4,137,1]{2,1,0:T(8,128)}, f32[4,137,1]{2,1,0:T(8,128)S(1)}, u32[]{:S(2)}, u32[]{:S(2)}) %collective-permute-start.16) | collective-permute-done | bytes 2224 | tf_op jit(solution)/shard_map/ppermute | solution.py:15
  143.7 7.2 %collective-permute-done.17 = f32[4,137,1]{2,1,0:T(8,128)S(1)} collective-permute-done((f32[4,137,1]{2,1,0:T(8,128)}, f32[4,137,1]{2,1,0:T(8,128)S(1)}, u32[]{:S(2)}, u32[]{:S(2)}) %collective-permute-start.17) | collective-permute-done | bytes 2224 | tf_op jit(solution)/shard_map/ppermute | solution.py:14
  153.4 3.2 %all-to-all-start.3 = ((f32[1,1,4,128]{3,1,0,2:T(1,128)}), f32[1,1,4,128]{3,1,0,2:T(1,128)S(1)}, u32[]{:S(2)}, u32[]{:S(2)}) async-start(f32[1,1,4,128]{3,1,0,2:T(1,128)} %bitcast.58), calls=%async_computation.3 | async-start | bytes 4096 | tf_op jit(solution)/shard_map/all_to_all | solution.py:89
  156.9 10.0 %all-to-all-done.3 = f32[1,1,4,128]{3,1,0,2:T(1,128)S(1)} async-done(((f32[1,1,4,128]{3,1,0,2:T(1,128)}), f32[1,1,4,128]{3,1,0,2:T(1,128)S(1)}, u32[]{:S(2)}, u32[]{:S(2)}) %all-to-all-start.3) | async-done | bytes 2080 | tf_op jit(solution)/shard_map/all_to_all | solution.py:89
  169.2 48.6 %all-reduce = (f32[]{:T(128)}, f32[]{:T(128)}) all-reduce(f32[]{:T(128)S(6)} %mul.422, f32[]{:T(128)} %get-tuple-element.12), channel_id=1, replica_groups=mesh['tm'=8,'space'=4] {'tm','space'}, use_global_device_ids=true, to_apply=%region_2.3 | all-reduce | flops 2 | bytes 16 | tf_op jit(solution)/shard_map/psum | solution.py:87
  (125 shorter events, 43.6 us)
Async XLA Ops:
  1.9 14.3 %all-to-all-start.1 = ((s32[1,1,4]{1,0,2:T(1,128)}), s32[1,1,4]{1,0,2:T(1,128)S(1)}, u32[]{:S(2)}, u32[]{:S(2)}) async-start(s32[1,1,4]{1,0,2:T(1,128)} %copy.83), calls=%async_computation.1 | async-start | bytes 4096 | tf_op jit(solution)/shard_map/all_to_all | solution.py:36
  8.3 23.9 %collective-permute-start = (f32[4,137,1]{1,2,0:T(1,128)S(1)}, f32[4,137,1]{1,2,0:T(1,128)S(1)}, u32[]{:S(2)}, u32[]{:S(2)}) collective-permute-start(f32[4,137,1]{1,2,0:T(1,128)S(1)} %get-tuple-element.45), channel_id=1, source_target_pairs={{0,1},{1,2},{2,3},{3,0},{4,5},{5,6},{6,7},{7,4},{8,9},{9,10},{10,1... | collective-permute-start | bytes 6584 | tf_op jit(solution)/shard_map/ppermute | solution.py:14
  10.4 21.8 %collective-permute-start.1 = (f32[4,137,1]{1,2,0:T(1,128)S(1)}, f32[4,137,1]{1,2,0:T(1,128)S(1)}, u32[]{:S(2)}, u32[]{:S(2)}) collective-permute-start(f32[4,137,1]{1,2,0:T(1,128)S(1)} %get-tuple-element.46), channel_id=1, source_target_pairs={{1,0},{2,1},{3,2},{0,3},{5,4},{6,5},{7,6},{4,7},{9,8},{10,9},{11,1... | collective-permute-start | bytes 6584 | tf_op jit(solution)/shard_map/ppermute | solution.py:15
  13.2 6.3 %copy-start.10 = (f32[1,1,4,3,128]{4,2,3,1,0:T(4,128)S(1)}, f32[1,1,4,3,128]{4,2,3,1,0:T(4,128)}, u32[]{:S(2)}) copy-start(f32[1,1,4,3,128]{4,2,3,1,0:T(4,128)} %param.10) | copy-start | bytes 18436
  13.2 19.4 %collective-permute-start.2 = (f32[4,137,1]{2,1,0:T(8,128)}, f32[4,137,1]{2,1,0:T(8,128)S(1)}, u32[]{:S(2)}, u32[]{:S(2)}) collective-permute-start(f32[4,137,1]{2,1,0:T(8,128)} %get-tuple-element.61), channel_id=1, source_target_pairs={{0,1},{1,2},{2,3},{3,0},{4,5},{5,6},{6,7},{7,4},{8,9},{9,10},{10,1... | collective-permute-start | bytes 6584 | tf_op jit(solution)/shard_map/ppermute | solution.py:14
  14.3 18.4 %collective-permute-start.3 = (f32[4,137,1]{2,1,0:T(8,128)}, f32[4,137,1]{2,1,0:T(8,128)}, u32[]{:S(2)}, u32[]{:S(2)}) collective-permute-start(f32[4,137,1]{2,1,0:T(8,128)} %get-tuple-element.62), channel_id=1, source_target_pairs={{1,0},{2,1},{3,2},{0,3},{5,4},{6,5},{7,6},{4,7},{9,8},{10,9},{11,1... | collective-permute-start | bytes 6584 | tf_op jit(solution)/shard_map/ppermute | solution.py:15
  16.2 12.7 %all-to-all-start.2 = ((s32[1,1,4,128]{3,1,0,2:T(1,128)}), s32[1,1,4,128]{3,1,0,2:T(1,128)S(1)}, u32[]{:S(2)}, u32[]{:S(2)}) async-start(s32[1,1,4,128]{3,1,0,2:T(1,128)} %bitcast.16), calls=%async_computation.2 | async-start | bytes 4096 | tf_op jit(solution)/shard_map/all_to_all | solution.py:34
  20.2 59.1 %copy-start.4 = (f32[137,128]{1,0:T(8,128)}, f32[137,128]{1,0:T(8,128)S(1)}, u32[]{:S(2)}) copy-start(f32[137,128]{1,0:T(8,128)S(1)} %copy.69) | copy-start | bytes 210436
  20.5 46.1 %copy-start.2 = (f32[137,128]{1,0:T(8,128)}, f32[137,128]{1,0:T(8,128)S(1)}, u32[]{:S(2)}) copy-start(f32[137,128]{1,0:T(8,128)S(1)} %copy.70) | copy-start | bytes 210436
  28.9 42.1 %all-to-all-start = ((f32[1,1,4,3,128]{4,3,1,0,2:T(4,128)}), f32[1,1,4,3,128]{4,3,1,0,2:T(4,128)S(1)}, u32[]{:S(2)}, u32[]{:S(2)}) async-start(f32[1,1,4,3,128]{4,3,1,0,2:T(4,128)} %copy.81), calls=%async_computation | async-start | bytes 16384 | tf_op jit(solution)/shard_map/all_to_all | solution.py:35
  34.1 10.8 %collective-permute-start.4 = (f32[4,137,1]{2,1,0:T(8,128)S(1)}, f32[4,137,1]{2,1,0:T(8,128)S(1)}, u32[]{:S(2)}, u32[]{:S(2)}) collective-permute-start(f32[4,137,1]{2,1,0:T(8,128)S(1)} %get-tuple-element.59), channel_id=1, source_target_pairs={{0,1},{1,2},{2,3},{3,0},{4,5},{5,6},{6,7},{7,4},{8,9},{9,10},{10,1... | collective-permute-start | bytes 6584 | tf_op jit(solution)/shard_map/ppermute | solution.py:14
  36.1 12.3 %collective-permute-start.5 = (f32[4,137,1]{2,1,0:T(8,128)S(1)}, f32[4,137,1]{2,1,0:T(8,128)}, u32[]{:S(2)}, u32[]{:S(2)}) collective-permute-start(f32[4,137,1]{2,1,0:T(8,128)S(1)} %get-tuple-element.60), channel_id=1, source_target_pairs={{1,0},{2,1},{3,2},{0,3},{5,4},{6,5},{7,6},{4,7},{9,8},{10,9},{11,1... | collective-permute-start | bytes 6584 | tf_op jit(solution)/shard_map/ppermute | solution.py:15
  50.6 16.0 %collective-permute-start.6 = (f32[4,137,1]{2,1,0:T(8,128)}, f32[4,137,1]{2,1,0:T(8,128)S(1)}, u32[]{:S(2)}, u32[]{:S(2)}) collective-permute-start(f32[4,137,1]{2,1,0:T(8,128)} %get-tuple-element.57), channel_id=1, source_target_pairs={{0,1},{1,2},{2,3},{3,0},{4,5},{5,6},{6,7},{7,4},{8,9},{9,10},{10,1... | collective-permute-start | bytes 6584 | tf_op jit(solution)/shard_map/ppermute | solution.py:14
  52.1 14.5 %collective-permute-start.7 = (f32[4,137,1]{2,1,0:T(8,128)}, f32[4,137,1]{2,1,0:T(8,128)}, u32[]{:S(2)}, u32[]{:S(2)}) collective-permute-start(f32[4,137,1]{2,1,0:T(8,128)} %get-tuple-element.58), channel_id=1, source_target_pairs={{1,0},{2,1},{3,2},{0,3},{5,4},{6,5},{7,6},{4,7},{9,8},{10,9},{11,1... | collective-permute-start | bytes 6584 | tf_op jit(solution)/shard_map/ppermute | solution.py:15
  68.1 9.3 %collective-permute-start.8 = (f32[4,137,1]{2,1,0:T(8,128)S(1)}, f32[4,137,1]{2,1,0:T(8,128)S(1)}, u32[]{:S(2)}, u32[]{:S(2)}) collective-permute-start(f32[4,137,1]{2,1,0:T(8,128)S(1)} %get-tuple-element.55), channel_id=1, source_target_pairs={{0,1},{1,2},{2,3},{3,0},{4,5},{5,6},{6,7},{7,4},{8,9},{9,10},{10,1... | collective-permute-start | bytes 6584 | tf_op jit(solution)/shard_map/ppermute | solution.py:14
  68.7 10.7 %collective-permute-start.9 = (f32[4,137,1]{2,1,0:T(8,128)S(1)}, f32[4,137,1]{2,1,0:T(8,128)S(1)}, u32[]{:S(2)}, u32[]{:S(2)}) collective-permute-start(f32[4,137,1]{2,1,0:T(8,128)S(1)} %get-tuple-element.56), channel_id=1, source_target_pairs={{1,0},{2,1},{3,2},{0,3},{5,4},{6,5},{7,6},{4,7},{9,8},{10,9},{11,1... | collective-permute-start | bytes 6584 | tf_op jit(solution)/shard_map/ppermute | solution.py:15
  86.0 10.0 %collective-permute-start.10 = (f32[4,137,128]{2,1,0:T(8,128)S(1)}, f32[4,137,128]{2,1,0:T(8,128)S(1)}, u32[]{:S(2)}, u32[]{:S(2)}) collective-permute-start(f32[4,137,128]{2,1,0:T(8,128)S(1)} %fusion.23), channel_id=1, source_target_pairs={{0,4},{4,8},{8,12},{12,16},{16,20},{20,24},{24,28},{1,5},{5,9},{9,... | collective-permute-start | bytes 841736 | tf_op jit(solution)/shard_map/ppermute | solution.py:23
  92.2 3.7 %copy-start = (f32[1,4,137,128]{3,1,2,0:T(4,128)S(1)}, f32[1,4,137,128]{3,1,2,0:T(4,128)}, u32[]{:S(2)}) copy-start(f32[1,4,137,128]{3,1,2,0:T(4,128)} %param.6) | copy-start | bytes 841732
  96.8 5.6 %collective-permute-start.11 = (f32[4,137,128]{2,1,0:T(8,128)}, f32[4,137,128]{2,1,0:T(8,128)}, u32[]{:S(2)}, u32[]{:S(2)}) collective-permute-start(f32[4,137,128]{2,1,0:T(8,128)} %broadcast_multiply_fusion), channel_id=1, source_target_pairs={{4,0},{8,4},{12,8},{16,12},{20,16},{24,20},{28,24},{5,1},{9,5},{13... | collective-permute-start | bytes 841736 | tf_op jit(solution)/shard_map/ppermute | solution.py:23
  104.3 7.0 %collective-permute-start.12 = (f32[4,137,1]{2,1,0:T(8,128)}, f32[4,137,1]{2,1,0:T(8,128)}, u32[]{:S(2)}, u32[]{:S(2)}) collective-permute-start(f32[4,137,1]{2,1,0:T(8,128)} %get-tuple-element.53), channel_id=1, source_target_pairs={{1,0},{2,1},{3,2},{0,3},{5,4},{6,5},{7,6},{4,7},{9,8},{10,9},{11,1... | collective-permute-start | bytes 6584 | tf_op jit(solution)/shard_map/ppermute | solution.py:15
  105.6 12.0 %collective-permute-start.13 = (f32[4,137,1]{2,1,0:T(8,128)}, f32[4,137,1]{2,1,0:T(8,128)}, u32[]{:S(2)}, u32[]{:S(2)}) collective-permute-start(f32[4,137,1]{2,1,0:T(8,128)} %get-tuple-element.54), channel_id=1, source_target_pairs={{0,1},{1,2},{2,3},{3,0},{4,5},{5,6},{6,7},{7,4},{8,9},{9,10},{10,1... | collective-permute-start | bytes 6584 | tf_op jit(solution)/shard_map/ppermute | solution.py:14
  107.2 10.4 %copy-start.5 = (f32[137,128]{1,0:T(8,128)S(1)}, f32[137,128]{1,0:T(8,128)}, u32[]{:S(2)}) copy-start(f32[137,128]{1,0:T(8,128)} %copy-done.4) | copy-start | bytes 210436
  108.4 13.5 %copy-start.8 = (f32[137,130]{0,1:T(8,128)S(1)}, f32[137,130]{0,1:T(8,128)}, u32[]{:S(2)}) copy-start(f32[137,130]{0,1:T(8,128)} %get-tuple-element.29) | copy-start | bytes 213724
  119.0 14.4 %copy-start.3 = (f32[137,128]{1,0:T(8,128)S(1)}, f32[137,128]{1,0:T(8,128)}, u32[]{:S(2)}) copy-start(f32[137,128]{1,0:T(8,128)} %copy-done.2) | copy-start | bytes 210436
  119.9 7.0 %collective-permute-start.14 = (f32[4,137,1]{2,1,0:T(8,128)}, f32[4,137,1]{2,1,0:T(8,128)S(1)}, u32[]{:S(2)}, u32[]{:S(2)}) collective-permute-start(f32[4,137,1]{2,1,0:T(8,128)} %get-tuple-element.51), channel_id=1, source_target_pairs={{1,0},{2,1},{3,2},{0,3},{5,4},{6,5},{7,6},{4,7},{9,8},{10,9},{11,1... | collective-permute-start | bytes 6584 | tf_op jit(solution)/shard_map/ppermute | solution.py:15
  120.2 13.2 %collective-permute-start.15 = (f32[4,137,1]{2,1,0:T(8,128)}, f32[4,137,1]{2,1,0:T(8,128)}, u32[]{:S(2)}, u32[]{:S(2)}) collective-permute-start(f32[4,137,1]{2,1,0:T(8,128)} %get-tuple-element.52), channel_id=1, source_target_pairs={{0,1},{1,2},{2,3},{3,0},{4,5},{5,6},{6,7},{7,4},{8,9},{9,10},{10,1... | collective-permute-start | bytes 6584 | tf_op jit(solution)/shard_map/ppermute | solution.py:14
  122.2 15.4 %copy-start.6 = (f32[137,130]{0,1:T(8,128)S(1)}, f32[137,130]{0,1:T(8,128)}, u32[]{:S(2)}) copy-start(f32[137,130]{0,1:T(8,128)} %get-tuple-element.28) | copy-start | bytes 213724
  135.6 8.1 %collective-permute-start.16 = (f32[4,137,1]{2,1,0:T(8,128)}, f32[4,137,1]{2,1,0:T(8,128)S(1)}, u32[]{:S(2)}, u32[]{:S(2)}) collective-permute-start(f32[4,137,1]{2,1,0:T(8,128)} %get-tuple-element.49), channel_id=1, source_target_pairs={{1,0},{2,1},{3,2},{0,3},{5,4},{6,5},{7,6},{4,7},{9,8},{10,9},{11,1... | collective-permute-start | bytes 6584 | tf_op jit(solution)/shard_map/ppermute | solution.py:15
  136.8 14.1 %collective-permute-start.17 = (f32[4,137,1]{2,1,0:T(8,128)}, f32[4,137,1]{2,1,0:T(8,128)S(1)}, u32[]{:S(2)}, u32[]{:S(2)}) collective-permute-start(f32[4,137,1]{2,1,0:T(8,128)} %get-tuple-element.50), channel_id=1, source_target_pairs={{0,1},{1,2},{2,3},{3,0},{4,5},{5,6},{6,7},{7,4},{8,9},{9,10},{10,1... | collective-permute-start | bytes 6584 | tf_op jit(solution)/shard_map/ppermute | solution.py:14
  151.4 15.6 %collective-permute-start.18 = (f32[4,137,1]{2,1,0:T(8,128)S(1)}, f32[4,137,1]{2,1,0:T(8,128)S(1)}, u32[]{:S(2)}, u32[]{:S(2)}) collective-permute-start(f32[4,137,1]{2,1,0:T(8,128)S(1)} %get-tuple-element.47), channel_id=1, source_target_pairs={{1,0},{2,1},{3,2},{0,3},{5,4},{6,5},{7,6},{4,7},{9,8},{10,9},{11,1... | collective-permute-start | bytes 6584 | tf_op jit(solution)/shard_map/ppermute | solution.py:15
  151.7 15.2 %collective-permute-start.19 = (f32[4,137,1]{2,1,0:T(8,128)S(1)}, f32[4,137,1]{2,1,0:T(8,128)S(1)}, u32[]{:S(2)}, u32[]{:S(2)}) collective-permute-start(f32[4,137,1]{2,1,0:T(8,128)S(1)} %get-tuple-element.48), channel_id=1, source_target_pairs={{0,1},{1,2},{2,3},{3,0},{4,5},{5,6},{6,7},{7,4},{8,9},{9,10},{10,1... | collective-permute-start | bytes 6584 | tf_op jit(solution)/shard_map/ppermute | solution.py:14
  153.4 13.5 %all-to-all-start.3 = ((f32[1,1,4,128]{3,1,0,2:T(1,128)}), f32[1,1,4,128]{3,1,0,2:T(1,128)S(1)}, u32[]{:S(2)}, u32[]{:S(2)}) async-start(f32[1,1,4,128]{3,1,0,2:T(1,128)} %bitcast.58), calls=%async_computation.3 | async-start | bytes 4096 | tf_op jit(solution)/shard_map/all_to_all | solution.py:89
  (3 other events, 9.6 us)
where the time goes:
time: 221 us
  waiting for transfers between devices  67.2 us (30%)
  blocking collectives  48.6 us (22%)
  local copies, waits for them, and re-layouts  41.5 us (19%)
  starting transfers between devices  40.5 us (18%)
  other arithmetic  18.9 us (9%)
  between operations  4 us (2%)
    psum x1, blocking collectives, on_device(): cost, norm = lax.psum((cost_part, norm_part), ('tm', 'space'))  48.6 us
    ppermute x9, waiting for transfers between devices, padded_2(): before = lax.ppermute(last, axis, up)  27.5 us
    gather x8, local copies, waits for them, and re-layouts, on_device(): seen = weight * line[flat] + (1.0 - weight) * line[flat + 1]  25.1 us
    ppermute x9, waiting for transfers between devices, padded_2(): after = lax.ppermute(initial, axis, down)  19 us
    ppermute x9, starting transfers between devices, padded_2(): before = lax.ppermute(last, axis, up)  12.2 us
    ppermute x9, starting transfers between devices, padded_2(): after = lax.ppermute(initial, axis, down)  10.8 us
    all_to_all x1, waiting for transfers between devices, on_device(): lax.all_to_all(departed[None, None], 'space', split_axis=2, concat_axis=2...  10 us
    all_to_all x1, waiting for transfers between devices, on_device(): lax.all_to_all(obs_code, 'space', split_axis=2, concat_axis=2, tiled=True)  8.22 us
  transfers between devices with their start and end apart: 24, of which 12 were waited for; matrix products, arithmetic and copies ran while one was open for 19% of the time, Pallas kernels for 0%

commit v1 on v0

--- a/solution.py
+++ b/solution.py
@@ -2,6 +2,10 @@
 import jax.numpy as jnp
 from jax import lax
 from jax.sharding import PartitionSpec as P
+
+group_perform = lambda in_array, bus_axis, axis_id: lax.psum(
+    lax.psum(in_array, axis_name=bus_axis), axis_name=axis_id
+)
 
 
 def padded_2(array, sides, width):
@@ -84,7 +88,7 @@
     gradient = weighted_own + lam
     cost_part = 0.5 * (jump_part + jnp.sum(pushed * departed))
     norm_part = jnp.sum(gradient * gradient)
-    cost, norm = lax.psum((cost_part, norm_part), ("tm", "space"))
+    cost, norm = group_perform((cost_part, norm_part), "space", "tm")
     renewed = increment - cost / norm * gradient[None]
     returned = lax.all_to_all(
         departed[None, None], "space", split_axis=2, concat_axis=2, tiled=True

time: 221 us -> 203 us (0.919)
  blocking collectives: 48.6 us -> 30 us
    psum x1 -> x2, blocking collectives: 48.6 us -> 30 us  [the longest x1 20.6 us: lax.psum(lax.psum(in_array, axis_name=bus_axis), axis_name=axis_id)]
  transfers between devices with their start and end apart: 24 -> 24, of which waited for: 12 -> 12; matrix products, arithmetic and copies ran while one was open for 19% -> 21% of each run, Pallas kernels for 0% -> 0%
where the time goes in v1:
time: 203 us; the launch traced here: 202 us
  waiting for transfers between devices  67.2 us (33%)
  local copies, waits for them, and re-layouts  41.5 us (20%)
  starting transfers between devices  40.5 us (20%)
  blocking collectives  30 us (15%)
  other arithmetic  18.9 us (9%)
  between operations  3.95 us (2%)
    ppermute x9, waiting for transfers between devices, padded_2(): before = lax.ppermute(last, axis, up)  27.5 us
    gather x8, local copies, waits for them, and re-layouts, on_device(): seen = weight * line[flat] + (1.0 - weight) * line[flat + 1]  25.1 us
    psum x1, blocking collectives, lax.psum(lax.psum(in_array, axis_name=bus_axis), axis_name=axis_id)  20.6 us
    ppermute x9, waiting for transfers between devices, padded_2(): after = lax.ppermute(initial, axis, down)  19 us
    ppermute x9, starting transfers between devices, padded_2(): before = lax.ppermute(last, axis, up)  12.2 us
    ppermute x9, starting transfers between devices, padded_2(): after = lax.ppermute(initial, axis, down)  10.8 us
    all_to_all x1, waiting for transfers between devices, on_device(): lax.all_to_all(departed[None, None], 'space', split_axis=2, concat_axis=2...  10 us
    psum x1, blocking collectives, lax.psum(in_array, axis_name=bus_axis)  9.34 us
  transfers between devices with their start and end apart: 24, of which 12 were waited for; matrix products, arithmetic and copies ran while one was open for 21% of the time, Pallas kernels for 0%

profile of v1, /device:TPU:0, one launch (start us, length us, event | category | flops | bytes accessed | tf_op | source)
XLA Modules:
  0.0 201.9 jit_solution(11366981946119428635)
XLA Ops:
  1.9 5.2 %all-to-all-start.1 = ((s32[1,1,4]{1,0,2:T(1,128)}), s32[1,1,4]{1,0,2:T(1,128)S(1)}, u32[]{:S(2)}, u32[]{:S(2)}) async-start(s32[1,1,4]{1,0,2:T(1,128)} %copy.83), calls=%async_computation.1 | async-start | bytes 4096 | tf_op jit(solution)/shard_map/all_to_all | solution.py:40
  8.3 2.1 %collective-permute-start = (f32[4,137,1]{1,2,0:T(1,128)S(1)}, f32[4,137,1]{1,2,0:T(1,128)S(1)}, u32[]{:S(2)}, u32[]{:S(2)}) collective-permute-start(f32[4,137,1]{1,2,0:T(1,128)S(1)} %get-tuple-element.47), channel_id=1, source_target_pairs={{0,1},{1,2},{2,3},{3,0},{4,5},{5,6},{6,7},{7,4},{8,9},{9,10},{10,1... | collective-permute-start | bytes 6584 | tf_op jit(solution)/shard_map/ppermute | solution.py:18
  14.3 1.9 collective-permute-start.3
  16.2 3.2 %all-to-all-start.2 = ((s32[1,1,4,128]{3,1,0,2:T(1,128)}), s32[1,1,4,128]{3,1,0,2:T(1,128)S(1)}, u32[]{:S(2)}, u32[]{:S(2)}) async-start(s32[1,1,4,128]{3,1,0,2:T(1,128)} %bitcast.16), calls=%async_computation.2 | async-start | bytes 4096 | tf_op jit(solution)/shard_map/all_to_all | solution.py:38
  20.7 8.2 %all-to-all-done.2 = s32[1,1,4,128]{3,1,0,2:T(1,128)S(1)} async-done(((s32[1,1,4,128]{3,1,0,2:T(1,128)}), s32[1,1,4,128]{3,1,0,2:T(1,128)S(1)}, u32[]{:S(2)}, u32[]{:S(2)}) %all-to-all-start.2) | async-done | bytes 2080 | tf_op jit(solution)/shard_map/all_to_all | solution.py:38
  28.9 3.2 %all-to-all-start = ((f32[1,1,4,3,128]{4,3,1,0,2:T(4,128)}), f32[1,1,4,3,128]{4,3,1,0,2:T(4,128)S(1)}, u32[]{:S(2)}, u32[]{:S(2)}) async-start(f32[1,1,4,3,128]{4,3,1,0,2:T(4,128)} %copy.81), calls=%async_computation | async-start | bytes 16384 | tf_op jit(solution)/shard_map/all_to_all | solution.py:39
  34.1 2.0 %collective-permute-start.4 = (f32[4,137,1]{2,1,0:T(8,128)S(1)}, f32[4,137,1]{2,1,0:T(8,128)S(1)}, u32[]{:S(2)}, u32[]{:S(2)}) collective-permute-start(f32[4,137,1]{2,1,0:T(8,128)S(1)} %get-tuple-element.61), channel_id=1, source_target_pairs={{0,1},{1,2},{2,3},{3,0},{4,5},{5,6},{6,7},{7,4},{8,9},{9,10},{10,1... | collective-permute-start | bytes 6584 | tf_op jit(solution)/shard_map/ppermute | solution.py:18
  37.3 7.6 %collective-permute-done.4 = f32[4,137,1]{2,1,0:T(8,128)S(1)} collective-permute-done((f32[4,137,1]{2,1,0:T(8,128)S(1)}, f32[4,137,1]{2,1,0:T(8,128)S(1)}, u32[]{:S(2)}, u32[]{:S(2)}) %collective-permute-start.4) | collective-permute-done | bytes 2224 | tf_op jit(solution)/shard_map/ppermute | solution.py:18
  44.9 3.5 %collective-permute-done.5 = f32[4,137,1]{2,1,0:T(8,128)} collective-permute-done((f32[4,137,1]{2,1,0:T(8,128)S(1)}, f32[4,137,1]{2,1,0:T(8,128)}, u32[]{:S(2)}, u32[]{:S(2)}) %collective-permute-start.5) | collective-permute-done | bytes 2224 | tf_op jit(solution)/shard_map/ppermute | solution.py:19
  54.0 3.1 %gather_fusion.7 = f32[512]{0:T(512)S(1)} fusion(f32[70144]{0:T(1024)S(1)} %reshape.355, s32[1024]{0:T(1024)S(1)} %get-tuple-element.74), kind=kCustom, calls=%fused_computation.7 | custom fusion | bytes 6144 | tf_op jit(solution)/shard_map/gather | solution.py:65
  57.1 3.1 %gather_fusion.6 = f32[512]{0:T(512)S(1)} fusion(f32[70144]{0:T(1024)S(1)} %reshape.355, s32[1024]{0:T(1024)S(1)} %get-tuple-element.75), kind=kCustom, calls=%fused_computation.6 | custom fusion | bytes 6144 | tf_op jit(solution)/shard_map/gather | solution.py:65
  60.3 3.1 %gather_fusion.5 = f32[512]{0:T(512)S(1)} fusion(f32[70144]{0:T(1024)S(1)} %reshape.354, s32[1024]{0:T(1024)S(1)} %get-tuple-element.74), kind=kCustom, calls=%fused_computation.5 | custom fusion | bytes 6144 | tf_op jit(solution)/shard_map/gather | solution.py:65
  63.4 3.1 %gather_fusion.4 = f32[512]{0:T(512)S(1)} fusion(f32[70144]{0:T(1024)S(1)} %reshape.354, s32[1024]{0:T(1024)S(1)} %get-tuple-element.75), kind=kCustom, calls=%fused_computation.4 | custom fusion | bytes 6144 | tf_op jit(solution)/shard_map/gather | solution.py:65
  68.6 2.4 %collective-permute-start.9 = (f32[4,137,1]{2,1,0:T(8,128)S(1)}, f32[4,137,1]{2,1,0:T(8,128)S(1)}, u32[]{:S(2)}, u32[]{:S(2)}) collective-permute-start(f32[4,137,1]{2,1,0:T(8,128)S(1)} %get-tuple-element.58), channel_id=1, source_target_pairs={{1,0},{2,1},{3,2},{0,3},{5,4},{6,5},{7,6},{4,7},{9,8},{10,9},{11,1... | collective-permute-start | bytes 6584 | tf_op jit(solution)/shard_map/ppermute | solution.py:19
  71.0 3.1 %gather_fusion.3 = f32[512]{0:T(512)S(1)} fusion(f32[70144]{0:T(1024)S(1)} %reshape.353, s32[1024]{0:T(1024)S(1)} %get-tuple-element.74), kind=kCustom, calls=%fused_computation.3 | custom fusion | bytes 6144 | tf_op jit(solution)/shard_map/gather | solution.py:65
  74.2 3.1 %gather_fusion.2 = f32[512]{0:T(512)S(1)} fusion(f32[70144]{0:T(1024)S(1)} %reshape.353, s32[1024]{0:T(1024)S(1)} %get-tuple-element.75), kind=kCustom, calls=%fused_computation.2 | custom fusion | bytes 6144 | tf_op jit(solution)/shard_map/gather | solution.py:65
  77.4 1.9 collective-permute-done.9
  79.6 3.1 %gather_fusion.1 = f32[512]{0:T(512)S(1)} fusion(f32[70144]{0:T(1024)S(1)} %reshape.352, s32[1024]{0:T(1024)S(1)} %get-tuple-element.74), kind=kCustom, calls=%fused_computation.1 | custom fusion | bytes 6144 | tf_op jit(solution)/shard_map/gather | solution.py:65
  82.8 3.1 %gather_fusion = f32[512]{0:T(512)S(1)} fusion(f32[70144]{0:T(1024)S(1)} %reshape.352, s32[1024]{0:T(1024)S(1)} %get-tuple-element.75), kind=kCustom, calls=%fused_computation | custom fusion | bytes 6144 | tf_op jit(solution)/shard_map/gather | solution.py:65
  88.7 3.5 %scatter_custom_fusion = f32[280576]{0:T(1024)S(1)} fusion(s32[512]{0:T(512)S(1)} %fusion.42, f32[512]{0:T(512)S(1)} %get-tuple-element.69, f32[]{:T(128)} %constant.16.clone.1), kind=kCustom, calls=%fused_computation.10 | custom fusion | flops 512 | bytes 1122308 | tf_op jit(solution)/shard_map/scatter-add | solution.py:76
  92.2 3.7 %scatter_fusion = f32[280576]{0:T(1024)S(1)} fusion(f32[280576]{0:T(1024)S(1)} %scatter_custom_fusion, s32[512]{0:T(512)S(1)} %get-tuple-element.72, f32[512]{0:T(512)S(1)} %get-tuple-element.68), kind=kCustom, calls=%fused_computation.9 | custom fusion | flops 512 | bytes 8192 | tf_op jit(solution)/shard_map/scatter-add | solution.py:76
  100.0 2.4 %collective-permute-done.11 = f32[4,137,128]{2,1,0:T(8,128)} collective-permute-done((f32[4,137,128]{2,1,0:T(8,128)}, f32[4,137,128]{2,1,0:T(8,128)}, u32[]{:S(2)}, u32[]{:S(2)}) %collective-permute-start.11) | collective-permute-done | bytes 280608 | tf_op jit(solution)/shard_map/ppermute | solution.py:27
  108.4 3.0 %collective-permute-done.12 = f32[4,137,1]{2,1,0:T(8,128)} collective-permute-done((f32[4,137,1]{2,1,0:T(8,128)}, f32[4,137,1]{2,1,0:T(8,128)}, u32[]{:S(2)}, u32[]{:S(2)}) %collective-permute-start.12) | collective-permute-done | bytes 2224 | tf_op jit(solution)/shard_map/ppermute | solution.py:19
  111.4 6.2 %collective-permute-done.13 = f32[4,137,1]{2,1,0:T(8,128)} collective-permute-done((f32[4,137,1]{2,1,0:T(8,128)}, f32[4,137,1]{2,1,0:T(8,128)}, u32[]{:S(2)}, u32[]{:S(2)}) %collective-permute-start.13) | collective-permute-done | bytes 2224 | tf_op jit(solution)/shard_map/ppermute | solution.py:18
  122.2 4.7 %collective-permute-done.14 = f32[4,137,1]{2,1,0:T(8,128)S(1)} collective-permute-done((f32[4,137,1]{2,1,0:T(8,128)}, f32[4,137,1]{2,1,0:T(8,128)S(1)}, u32[]{:S(2)}, u32[]{:S(2)}) %collective-permute-start.14) | collective-permute-done | bytes 2224 | tf_op jit(solution)/shard_map/ppermute | solution.py:19
  127.0 6.5 %collective-permute-done.15 = f32[4,137,1]{2,1,0:T(8,128)} collective-permute-done((f32[4,137,1]{2,1,0:T(8,128)}, f32[4,137,1]{2,1,0:T(8,128)}, u32[]{:S(2)}, u32[]{:S(2)}) %collective-permute-start.15) | collective-permute-done | bytes 2224 | tf_op jit(solution)/shard_map/ppermute | solution.py:18
  137.9 5.8 %collective-permute-done.16 = f32[4,137,1]{2,1,0:T(8,128)S(1)} collective-permute-done((f32[4,137,1]{2,1,0:T(8,128)}, f32[4,137,1]{2,1,0:T(8,128)S(1)}, u32[]{:S(2)}, u32[]{:S(2)}) %collective-permute-start.16) | collective-permute-done | bytes 2224 | tf_op jit(solution)/shard_map/ppermute | solution.py:19
  143.7 7.2 %collective-permute-done.17 = f32[4,137,1]{2,1,0:T(8,128)S(1)} collective-permute-done((f32[4,137,1]{2,1,0:T(8,128)}, f32[4,137,1]{2,1,0:T(8,128)S(1)}, u32[]{:S(2)}, u32[]{:S(2)}) %collective-permute-start.17) | collective-permute-done | bytes 2224 | tf_op jit(solution)/shard_map/ppermute | solution.py:18
  153.4 3.2 %all-to-all-start.3 = ((f32[1,1,4,128]{3,1,0,2:T(1,128)}), f32[1,1,4,128]{3,1,0,2:T(1,128)S(1)}, u32[]{:S(2)}, u32[]{:S(2)}) async-start(f32[1,1,4,128]{3,1,0,2:T(1,128)} %bitcast.58), calls=%async_computation.3 | async-start | bytes 4096 | tf_op jit(solution)/shard_map/all_to_all | solution.py:93
  156.9 10.0 %all-to-all-done.3 = f32[1,1,4,128]{3,1,0,2:T(1,128)S(1)} async-done(((f32[1,1,4,128]{3,1,0,2:T(1,128)}), f32[1,1,4,128]{3,1,0,2:T(1,128)S(1)}, u32[]{:S(2)}, u32[]{:S(2)}) %all-to-all-start.3) | async-done | bytes 2080 | tf_op jit(solution)/shard_map/all_to_all | solution.py:93
  169.2 9.3 %all-reduce.1 = (f32[]{:T(128)}, f32[]{:T(128)}) all-reduce(f32[]{:T(128)S(6)} %mul.422, f32[]{:T(128)} %get-tuple-element.14), channel_id=1, replica_groups=mesh['tm'=8,'space'=4] {'space'}, use_global_device_ids=true, to_apply=%region_2.3 | all-reduce | flops 2 | bytes 16 | tf_op jit(solution)/shard_map/psum | solution.py:7
  178.5 20.6 %all-reduce = (f32[]{:T(128)}, f32[]{:T(128)}) all-reduce(f32[]{:T(128)} %get-tuple-element.10, f32[]{:T(128)} %get-tuple-element.11), channel_id=1, replica_groups=mesh['tm'=8,'space'=4] {'tm'}, use_global_device_ids=true, to_apply=%region_3.4 | all-reduce | flops 2 | bytes 16 | tf_op jit(solution)/shard_map/psum | solution.py:6
  (126 shorter events, 45.3 us)
Async XLA Ops:
  1.9 14.2 %all-to-all-start.1 = ((s32[1,1,4]{1,0,2:T(1,128)}), s32[1,1,4]{1,0,2:T(1,128)S(1)}, u32[]{:S(2)}, u32[]{:S(2)}) async-start(s32[1,1,4]{1,0,2:T(1,128)} %copy.83), calls=%async_computation.1 | async-start | bytes 4096 | tf_op jit(solution)/shard_map/all_to_all | solution.py:40
  8.3 23.9 %collective-permute-start = (f32[4,137,1]{1,2,0:T(1,128)S(1)}, f32[4,137,1]{1,2,0:T(1,128)S(1)}, u32[]{:S(2)}, u32[]{:S(2)}) collective-permute-start(f32[4,137,1]{1,2,0:T(1,128)S(1)} %get-tuple-element.47), channel_id=1, source_target_pairs={{0,1},{1,2},{2,3},{3,0},{4,5},{5,6},{6,7},{7,4},{8,9},{9,10},{10,1... | collective-permute-start | bytes 6584 | tf_op jit(solution)/shard_map/ppermute | solution.py:18
  10.4 21.8 %collective-permute-start.1 = (f32[4,137,1]{1,2,0:T(1,128)S(1)}, f32[4,137,1]{1,2,0:T(1,128)S(1)}, u32[]{:S(2)}, u32[]{:S(2)}) collective-permute-start(f32[4,137,1]{1,2,0:T(1,128)S(1)} %get-tuple-element.48), channel_id=1, source_target_pairs={{1,0},{2,1},{3,2},{0,3},{5,4},{6,5},{7,6},{4,7},{9,8},{10,9},{11,1... | collective-permute-start | bytes 6584 | tf_op jit(solution)/shard_map/ppermute | solution.py:19
  13.2 6.3 %copy-start.10 = (f32[1,1,4,3,128]{4,2,3,1,0:T(4,128)S(1)}, f32[1,1,4,3,128]{4,2,3,1,0:T(4,128)}, u32[]{:S(2)}) copy-start(f32[1,1,4,3,128]{4,2,3,1,0:T(4,128)} %param.10) | copy-start | bytes 18436
  13.2 19.4 %collective-permute-start.2 = (f32[4,137,1]{2,1,0:T(8,128)}, f32[4,137,1]{2,1,0:T(8,128)S(1)}, u32[]{:S(2)}, u32[]{:S(2)}) collective-permute-start(f32[4,137,1]{2,1,0:T(8,128)} %get-tuple-element.63), channel_id=1, source_target_pairs={{0,1},{1,2},{2,3},{3,0},{4,5},{5,6},{6,7},{7,4},{8,9},{9,10},{10,1... | collective-permute-start | bytes 6584 | tf_op jit(solution)/shard_map/ppermute | solution.py:18
  14.3 18.4 %collective-permute-start.3 = (f32[4,137,1]{2,1,0:T(8,128)}, f32[4,137,1]{2,1,0:T(8,128)}, u32[]{:S(2)}, u32[]{:S(2)}) collective-permute-start(f32[4,137,1]{2,1,0:T(8,128)} %get-tuple-element.64), channel_id=1, source_target_pairs={{1,0},{2,1},{3,2},{0,3},{5,4},{6,5},{7,6},{4,7},{9,8},{10,9},{11,1... | collective-permute-start | bytes 6584 | tf_op jit(solution)/shard_map/ppermute | solution.py:19
  16.2 12.7 %all-to-all-start.2 = ((s32[1,1,4,128]{3,1,0,2:T(1,128)}), s32[1,1,4,128]{3,1,0,2:T(1,128)S(1)}, u32[]{:S(2)}, u32[]{:S(2)}) async-start(s32[1,1,4,128]{3,1,0,2:T(1,128)} %bitcast.16), calls=%async_computation.2 | async-start | bytes 4096 | tf_op jit(solution)/shard_map/all_to_all | solution.py:38
  20.2 59.1 %copy-start.4 = (f32[137,128]{1,0:T(8,128)}, f32[137,128]{1,0:T(8,128)S(1)}, u32[]{:S(2)}) copy-start(f32[137,128]{1,0:T(8,128)S(1)} %copy.69) | copy-start | bytes 210436
  20.5 46.1 %copy-start.2 = (f32[137,128]{1,0:T(8,128)}, f32[137,128]{1,0:T(8,128)S(1)}, u32[]{:S(2)}) copy-start(f32[137,128]{1,0:T(8,128)S(1)} %copy.70) | copy-start | bytes 210436
  28.9 42.1 %all-to-all-start = ((f32[1,1,4,3,128]{4,3,1,0,2:T(4,128)}), f32[1,1,4,3,128]{4,3,1,0,2:T(4,128)S(1)}, u32[]{:S(2)}, u32[]{:S(2)}) async-start(f32[1,1,4,3,128]{4,3,1,0,2:T(4,128)} %copy.81), calls=%async_computation | async-start | bytes 16384 | tf_op jit(solution)/shard_map/all_to_all | solution.py:39
  34.1 10.8 %collective-permute-start.4 = (f32[4,137,1]{2,1,0:T(8,128)S(1)}, f32[4,137,1]{2,1,0:T(8,128)S(1)}, u32[]{:S(2)}, u32[]{:S(2)}) collective-permute-start(f32[4,137,1]{2,1,0:T(8,128)S(1)} %get-tuple-element.61), channel_id=1, source_target_pairs={{0,1},{1,2},{2,3},{3,0},{4,5},{5,6},{6,7},{7,4},{8,9},{9,10},{10,1... | collective-permute-start | bytes 6584 | tf_op jit(solution)/shard_map/ppermute | solution.py:18
  36.1 12.3 %collective-permute-start.5 = (f32[4,137,1]{2,1,0:T(8,128)S(1)}, f32[4,137,1]{2,1,0:T(8,128)}, u32[]{:S(2)}, u32[]{:S(2)}) collective-permute-start(f32[4,137,1]{2,1,0:T(8,128)S(1)} %get-tuple-element.62), channel_id=1, source_target_pairs={{1,0},{2,1},{3,2},{0,3},{5,4},{6,5},{7,6},{4,7},{9,8},{10,9},{11,1... | collective-permute-start | bytes 6584 | tf_op jit(solution)/shard_map/ppermute | solution.py:19
  50.6 16.0 %collective-permute-start.6 = (f32[4,137,1]{2,1,0:T(8,128)}, f32[4,137,1]{2,1,0:T(8,128)S(1)}, u32[]{:S(2)}, u32[]{:S(2)}) collective-permute-start(f32[4,137,1]{2,1,0:T(8,128)} %get-tuple-element.59), channel_id=1, source_target_pairs={{0,1},{1,2},{2,3},{3,0},{4,5},{5,6},{6,7},{7,4},{8,9},{9,10},{10,1... | collective-permute-start | bytes 6584 | tf_op jit(solution)/shard_map/ppermute | solution.py:18
  52.1 14.5 %collective-permute-start.7 = (f32[4,137,1]{2,1,0:T(8,128)}, f32[4,137,1]{2,1,0:T(8,128)}, u32[]{:S(2)}, u32[]{:S(2)}) collective-permute-start(f32[4,137,1]{2,1,0:T(8,128)} %get-tuple-element.60), channel_id=1, source_target_pairs={{1,0},{2,1},{3,2},{0,3},{5,4},{6,5},{7,6},{4,7},{9,8},{10,9},{11,1... | collective-permute-start | bytes 6584 | tf_op jit(solution)/shard_map/ppermute | solution.py:19
  68.0 9.3 %collective-permute-start.8 = (f32[4,137,1]{2,1,0:T(8,128)S(1)}, f32[4,137,1]{2,1,0:T(8,128)S(1)}, u32[]{:S(2)}, u32[]{:S(2)}) collective-permute-start(f32[4,137,1]{2,1,0:T(8,128)S(1)} %get-tuple-element.57), channel_id=1, source_target_pairs={{0,1},{1,2},{2,3},{3,0},{4,5},{5,6},{6,7},{7,4},{8,9},{9,10},{10,1... | collective-permute-start | bytes 6584 | tf_op jit(solution)/shard_map/ppermute | solution.py:18
  68.6 10.7 %collective-permute-start.9 = (f32[4,137,1]{2,1,0:T(8,128)S(1)}, f32[4,137,1]{2,1,0:T(8,128)S(1)}, u32[]{:S(2)}, u32[]{:S(2)}) collective-permute-start(f32[4,137,1]{2,1,0:T(8,128)S(1)} %get-tuple-element.58), channel_id=1, source_target_pairs={{1,0},{2,1},{3,2},{0,3},{5,4},{6,5},{7,6},{4,7},{9,8},{10,9},{11,1... | collective-permute-start | bytes 6584 | tf_op jit(solution)/shard_map/ppermute | solution.py:19
  85.9 10.0 %collective-permute-start.10 = (f32[4,137,128]{2,1,0:T(8,128)S(1)}, f32[4,137,128]{2,1,0:T(8,128)S(1)}, u32[]{:S(2)}, u32[]{:S(2)}) collective-permute-start(f32[4,137,128]{2,1,0:T(8,128)S(1)} %fusion.23), channel_id=1, source_target_pairs={{0,4},{4,8},{8,12},{12,16},{16,20},{20,24},{24,28},{1,5},{5,9},{9,... | collective-permute-start | bytes 841736 | tf_op jit(solution)/shard_map/ppermute | solution.py:27
  92.2 3.7 %copy-start = (f32[1,4,137,128]{3,1,2,0:T(4,128)S(1)}, f32[1,4,137,128]{3,1,2,0:T(4,128)}, u32[]{:S(2)}) copy-start(f32[1,4,137,128]{3,1,2,0:T(4,128)} %param.6) | copy-start | bytes 841732
  96.8 5.6 %collective-permute-start.11 = (f32[4,137,128]{2,1,0:T(8,128)}, f32[4,137,128]{2,1,0:T(8,128)}, u32[]{:S(2)}, u32[]{:S(2)}) collective-permute-start(f32[4,137,128]{2,1,0:T(8,128)} %broadcast_multiply_fusion), channel_id=1, source_target_pairs={{4,0},{8,4},{12,8},{16,12},{20,16},{24,20},{28,24},{5,1},{9,5},{13... | collective-permute-start | bytes 841736 | tf_op jit(solution)/shard_map/ppermute | solution.py:27
  104.4 7.0 %collective-permute-start.12 = (f32[4,137,1]{2,1,0:T(8,128)}, f32[4,137,1]{2,1,0:T(8,128)}, u32[]{:S(2)}, u32[]{:S(2)}) collective-permute-start(f32[4,137,1]{2,1,0:T(8,128)} %get-tuple-element.55), channel_id=1, source_target_pairs={{1,0},{2,1},{3,2},{0,3},{5,4},{6,5},{7,6},{4,7},{9,8},{10,9},{11,1... | collective-permute-start | bytes 6584 | tf_op jit(solution)/shard_map/ppermute | solution.py:19
  105.6 12.0 %collective-permute-start.13 = (f32[4,137,1]{2,1,0:T(8,128)}, f32[4,137,1]{2,1,0:T(8,128)}, u32[]{:S(2)}, u32[]{:S(2)}) collective-permute-start(f32[4,137,1]{2,1,0:T(8,128)} %get-tuple-element.56), channel_id=1, source_target_pairs={{0,1},{1,2},{2,3},{3,0},{4,5},{5,6},{6,7},{7,4},{8,9},{9,10},{10,1... | collective-permute-start | bytes 6584 | tf_op jit(solution)/shard_map/ppermute | solution.py:18
  107.2 10.4 %copy-start.5 = (f32[137,128]{1,0:T(8,128)S(1)}, f32[137,128]{1,0:T(8,128)}, u32[]{:S(2)}) copy-start(f32[137,128]{1,0:T(8,128)} %copy-done.4) | copy-start | bytes 210436
  108.4 13.5 %copy-start.8 = (f32[137,130]{0,1:T(8,128)S(1)}, f32[137,130]{0,1:T(8,128)}, u32[]{:S(2)}) copy-start(f32[137,130]{0,1:T(8,128)} %get-tuple-element.31) | copy-start | bytes 213724
  119.0 14.4 %copy-start.3 = (f32[137,128]{1,0:T(8,128)S(1)}, f32[137,128]{1,0:T(8,128)}, u32[]{:S(2)}) copy-start(f32[137,128]{1,0:T(8,128)} %copy-done.2) | copy-start | bytes 210436
  119.9 7.0 %collective-permute-start.14 = (f32[4,137,1]{2,1,0:T(8,128)}, f32[4,137,1]{2,1,0:T(8,128)S(1)}, u32[]{:S(2)}, u32[]{:S(2)}) collective-permute-start(f32[4,137,1]{2,1,0:T(8,128)} %get-tuple-element.53), channel_id=1, source_target_pairs={{1,0},{2,1},{3,2},{0,3},{5,4},{6,5},{7,6},{4,7},{9,8},{10,9},{11,1... | collective-permute-start | bytes 6584 | tf_op jit(solution)/shard_map/ppermute | solution.py:19
  120.2 13.2 %collective-permute-start.15 = (f32[4,137,1]{2,1,0:T(8,128)}, f32[4,137,1]{2,1,0:T(8,128)}, u32[]{:S(2)}, u32[]{:S(2)}) collective-permute-start(f32[4,137,1]{2,1,0:T(8,128)} %get-tuple-element.54), channel_id=1, source_target_pairs={{0,1},{1,2},{2,3},{3,0},{4,5},{5,6},{6,7},{7,4},{8,9},{9,10},{10,1... | collective-permute-start | bytes 6584 | tf_op jit(solution)/shard_map/ppermute | solution.py:18
  122.2 15.4 %copy-start.6 = (f32[137,130]{0,1:T(8,128)S(1)}, f32[137,130]{0,1:T(8,128)}, u32[]{:S(2)}) copy-start(f32[137,130]{0,1:T(8,128)} %get-tuple-element.30) | copy-start | bytes 213724
  135.6 8.1 %collective-permute-start.16 = (f32[4,137,1]{2,1,0:T(8,128)}, f32[4,137,1]{2,1,0:T(8,128)S(1)}, u32[]{:S(2)}, u32[]{:S(2)}) collective-permute-start(f32[4,137,1]{2,1,0:T(8,128)} %get-tuple-element.51), channel_id=1, source_target_pairs={{1,0},{2,1},{3,2},{0,3},{5,4},{6,5},{7,6},{4,7},{9,8},{10,9},{11,1... | collective-permute-start | bytes 6584 | tf_op jit(solution)/shard_map/ppermute | solution.py:19
  136.8 14.1 %collective-permute-start.17 = (f32[4,137,1]{2,1,0:T(8,128)}, f32[4,137,1]{2,1,0:T(8,128)S(1)}, u32[]{:S(2)}, u32[]{:S(2)}) collective-permute-start(f32[4,137,1]{2,1,0:T(8,128)} %get-tuple-element.52), channel_id=1, source_target_pairs={{0,1},{1,2},{2,3},{3,0},{4,5},{5,6},{6,7},{7,4},{8,9},{9,10},{10,1... | collective-permute-start | bytes 6584 | tf_op jit(solution)/shard_map/ppermute | solution.py:18
  151.3 15.6 %collective-permute-start.18 = (f32[4,137,1]{2,1,0:T(8,128)S(1)}, f32[4,137,1]{2,1,0:T(8,128)S(1)}, u32[]{:S(2)}, u32[]{:S(2)}) collective-permute-start(f32[4,137,1]{2,1,0:T(8,128)S(1)} %get-tuple-element.49), channel_id=1, source_target_pairs={{1,0},{2,1},{3,2},{0,3},{5,4},{6,5},{7,6},{4,7},{9,8},{10,9},{11,1... | collective-permute-start | bytes 6584 | tf_op jit(solution)/shard_map/ppermute | solution.py:19
  151.7 15.2 %collective-permute-start.19 = (f32[4,137,1]{2,1,0:T(8,128)S(1)}, f32[4,137,1]{2,1,0:T(8,128)S(1)}, u32[]{:S(2)}, u32[]{:S(2)}) collective-permute-start(f32[4,137,1]{2,1,0:T(8,128)S(1)} %get-tuple-element.50), channel_id=1, source_target_pairs={{0,1},{1,2},{2,3},{3,0},{4,5},{5,6},{6,7},{7,4},{8,9},{9,10},{10,1... | collective-permute-start | bytes 6584 | tf_op jit(solution)/shard_map/ppermute | solution.py:18
  153.4 13.5 %all-to-all-start.3 = ((f32[1,1,4,128]{3,1,0,2:T(1,128)}), f32[1,1,4,128]{3,1,0,2:T(1,128)S(1)}, u32[]{:S(2)}, u32[]{:S(2)}) async-start(f32[1,1,4,128]{3,1,0,2:T(1,128)} %bitcast.58), calls=%async_computation.3 | async-start | bytes 4096 | tf_op jit(solution)/shard_map/all_to_all | solution.py:93
  (3 other events, 9.6 us)
